TPU v7x, 256 devices: a whole 4x4x8 slice. The times are simulated.
256 devices in a mesh: ctx: 64 (over z, x, core), head: 4 (over y).
Axes of the slice: x: 4, y: 4, z: 8, core: 2. Of those that a mesh axis runs over, the one named last changes fastest.
Arguments:
- queries: bfloat16 [16384, 4096], P('ctx', 'head'), may hold values from -48 to 48
- keys: bfloat16 [16384, 1024], P('ctx', 'head'), may hold values from -48 to 48
- values: bfloat16 [16384, 1024], P('ctx', 'head'), may hold values from -6 to 6
- lengths: int32 [16], replicated, may hold values from 1 to 2048, 16384 in all
- out_weight: bfloat16 [4096, 4096], P('head'), may hold values from -0.09375 to 0.09375
Outputs:
- attended: bfloat16 [16384, 4096], P('ctx', 'head')
- log_sum: float32 [32, 16384], P('head', 'ctx')
- projected: bfloat16 [16384, 4096], P(('ctx', 'head'))
All inputs are finite; a program needn't handle non-finite values.
Results may differ from a plain program's by a relative error of at most 0.015.
Values may be sent and summed in bfloat16 or wider, within the bound.
A program may use at most 64 MiB of HBM per device.

v0:
```python
import jax
import jax.numpy as jnp
from jax import lax
from jax.sharding import PartitionSpec as P

HD = 128


def from_behind(block, axis, distance):
    devices = range(lax.axis_size(axis))
    route = [(i - distance, i) for i in devices if i - distance in devices]
    return lax.ppermute(block, axis, route)


def doc_index(positions, ends):
    return jnp.sum((ends[None, :] <= positions[:, None]).astype(jnp.int32), axis=1)


def local(queries, keys, values, lengths, out_weight):
    tok_rows = queries.shape[0]
    head_dim = HD
    kv_local = keys.shape[1] // head_dim
    q_local = queries.shape[1] // head_dim
    group = q_local // kv_local
    scale = head_dim ** (-0.5)
    all_tokens = tok_rows * lax.axis_size("ctx")
    longest = min(8 * tok_rows, all_tokens // 2)
    reach = (longest - 1) // tok_rows + 1
    ends = jnp.cumsum(lengths)
    base = lax.axis_index("ctx") * tok_rows
    qpos = base + jnp.arange(tok_rows, dtype=jnp.int32)
    qdoc = doc_index(qpos, ends)
    qheads = queries.reshape(tok_rows, kv_local, group, head_dim)

    def attend(state, block, kstart):
        kpos = kstart + jnp.arange(tok_rows, dtype=jnp.int32)
        kdoc = doc_index(kpos, ends)
        mask = (
            (kpos[None, :] <= qpos[:, None])
            & (kpos[None, :] >= 0)
            & (kdoc[None, :] == qdoc[:, None])
        )
        old_top, old_total, old_accum = state
        kh = block[0].reshape(tok_rows, kv_local, head_dim)
        vh = block[1].reshape(tok_rows, kv_local, head_dim)
        score = jnp.einsum("qgrd,kgd->grqk", qheads, kh, preferred_element_type=jnp.float32) * scale
        score = jnp.where(mask[None, None], score, -jnp.inf)
        new_top = jnp.maximum(old_top, jnp.max(score, axis=-1))
        correct = jnp.exp(old_top - new_top)
        expo = jnp.exp(score - new_top[..., None])
        new_total = old_total * correct + jnp.sum(expo, axis=-1)
        mixed = jnp.einsum(
            "grqk,kgd->qgrd", expo.astype(jnp.bfloat16), vh, preferred_element_type=jnp.float32
        )
        new_accum = old_accum * jnp.transpose(correct, (2, 0, 1))[..., None] + mixed
        return (new_top, new_total, new_accum)

    state = (
        jnp.full((kv_local, group, tok_rows), -1e30, jnp.float32),
        jnp.zeros((kv_local, group, tok_rows), jnp.float32),
        jnp.zeros((tok_rows, kv_local, group, head_dim), jnp.float32),
    )
    own = jnp.stack([keys, values], axis=0)
    state = attend(state, own, base)
    moving = own
    for step in range(1, reach + 1):
        moving = from_behind(moving, "ctx", 1)
        state = attend(state, moving, base - step * tok_rows)
    top, total, accum = state
    attended = (
        (accum / jnp.transpose(total, (2, 0, 1))[..., None])
        .reshape(tok_rows, q_local * head_dim)
        .astype(jnp.bfloat16)
    )
    log_sum = (top + jnp.log(total)).reshape(q_local, tok_rows)
    summed = lax.psum_scatter(
        jnp.dot(attended, out_weight, preferred_element_type=jnp.float32).astype(jnp.bfloat16),
        "head",
        scatter_dimension=0,
        tiled=True,
    )
    return (attended, log_sum, summed)


def solution(mesh):
    placed = (P("ctx", "head"), P("ctx", "head"), P("ctx", "head"), P(), P("head", None))
    return jax.shard_map(
        local,
        mesh=mesh,
        in_specs=placed,
        out_specs=(P("ctx", "head"), P("head", "ctx"), P(("ctx", "head"), None)),
        check_vma=False,
    )
```

profile of v0, /device:TPU:128, one launch (start us, length us, event | category | flops | bytes accessed | tf_op | source)
XLA Modules:
  0.0 149.4 jit_solution(16765309049684675498)
XLA Ops:
  7.2 0.0 reduce-scatter.2.cloned.1.call-start
  7.2 1.0 copy.131
  8.2 1.0 copy.75
  9.3 1.9 %collective-permute-start = (bf16[2,256,256]{1,2,0:T(8,128)(2,1)S(1)}, bf16[2,256,256]{1,2,0:T(8,128)(2,1)S(1)}, u32[]{:S(2)}, u32[]{:S(2)}) collective-permute-start(bf16[2,256,256]{1,2,0:T(8,128)(2,1)S(1)} %pad_maximum_fusion), channel_id=1, source_target_pairs={{0,4},{4,8},{8,12},{12,16},{16,20},{20,24},{24,28},{28,32},{32,36}... | collective-permute-start | bytes 786440 | tf_op jit(solution)/shard_map/ppermute | solution.py:12
  11.3 0.9 reshape_squeeze_stack.6
  12.3 0.7 copy.70
  13.1 0.1 reduce
  13.2 1.4 reshape.889
  14.6 0.1 convert_reduce_fusion
  14.7 0.9 compare_and_fusion.6
  15.6 0.5 fusion.97
  16.1 0.6 compare_and_fusion.1
  16.7 3.6 %collective-permute-done = bf16[2,256,256]{1,2,0:T(8,128)(2,1)S(1)} collective-permute-done((bf16[2,256,256]{1,2,0:T(8,128)(2,1)S(1)}, bf16[2,256,256]{1,2,0:T(8,128)(2,1)S(1)}, u32[]{:S(2)}, u32[]{:S(2)}) %collective-permute-start) | collective-permute-done | bytes 262176 | tf_op jit(solution)/shard_map/ppermute | solution.py:12
  20.3 1.9 %collective-permute-start.1 = (bf16[2,256,256]{1,2,0:T(8,128)(2,1)S(1)}, bf16[2,256,256]{1,2,0:T(8,128)(2,1)S(1)}, u32[]{:S(2)}, u32[]{:S(2)}) collective-permute-start(bf16[2,256,256]{1,2,0:T(8,128)(2,1)S(1)} %collective-permute-done), channel_id=1, source_target_pairs={{0,4},{4,8},{8,12},{12,16},{16,20},{20,24},{24,28},{28,32},{32,36}... | collective-permute-start | bytes 786440 | tf_op jit(solution)/shard_map/ppermute | solution.py:12
  22.2 0.6 fusion.96
  22.8 8.5 %collective-permute-done.1 = bf16[2,256,256]{1,2,0:T(8,128)(2,1)S(1)} collective-permute-done((bf16[2,256,256]{1,2,0:T(8,128)(2,1)S(1)}, bf16[2,256,256]{1,2,0:T(8,128)(2,1)S(1)}, u32[]{:S(2)}, u32[]{:S(2)}) %collective-permute-start.1) | collective-permute-done | bytes 262176 | tf_op jit(solution)/shard_map/ppermute | solution.py:12
  31.3 1.9 %collective-permute-start.2 = (bf16[2,256,256]{1,2,0:T(8,128)(2,1)S(1)}, bf16[2,256,256]{1,2,0:T(8,128)(2,1)S(1)}, u32[]{:S(2)}, u32[]{:S(2)}) collective-permute-start(bf16[2,256,256]{1,2,0:T(8,128)(2,1)S(1)} %collective-permute-done.1), channel_id=1, source_target_pairs={{0,4},{4,8},{8,12},{12,16},{16,20},{20,24},{24,28},{28,32},{32,36}... | collective-permute-start | bytes 786440 | tf_op jit(solution)/shard_map/ppermute | solution.py:12
  33.3 0.6 fusion.95
  33.8 8.5 %collective-permute-done.2 = bf16[2,256,256]{1,2,0:T(8,128)(2,1)S(1)} collective-permute-done((bf16[2,256,256]{1,2,0:T(8,128)(2,1)S(1)}, bf16[2,256,256]{1,2,0:T(8,128)(2,1)S(1)}, u32[]{:S(2)}, u32[]{:S(2)}) %collective-permute-start.2) | collective-permute-done | bytes 262176 | tf_op jit(solution)/shard_map/ppermute | solution.py:12
  42.4 1.9 %collective-permute-start.3 = (bf16[2,256,256]{1,2,0:T(8,128)(2,1)S(1)}, bf16[2,256,256]{1,2,0:T(8,128)(2,1)S(1)}, u32[]{:S(2)}, u32[]{:S(2)}) collective-permute-start(bf16[2,256,256]{1,2,0:T(8,128)(2,1)S(1)} %collective-permute-done.2), channel_id=1, source_target_pairs={{0,4},{4,8},{8,12},{12,16},{16,20},{20,24},{24,28},{28,32},{32,36}... | collective-permute-start | bytes 786440 | tf_op jit(solution)/shard_map/ppermute | solution.py:12
  44.3 0.6 fusion.94
  44.8 8.5 %collective-permute-done.3 = bf16[2,256,256]{1,2,0:T(8,128)(2,1)S(1)} collective-permute-done((bf16[2,256,256]{1,2,0:T(8,128)(2,1)S(1)}, bf16[2,256,256]{1,2,0:T(8,128)(2,1)S(1)}, u32[]{:S(2)}, u32[]{:S(2)}) %collective-permute-start.3) | collective-permute-done | bytes 262176 | tf_op jit(solution)/shard_map/ppermute | solution.py:12
  53.4 1.9 %collective-permute-start.4 = (bf16[2,256,256]{1,2,0:T(8,128)(2,1)S(1)}, bf16[2,256,256]{1,2,0:T(8,128)(2,1)S(1)}, u32[]{:S(2)}, u32[]{:S(2)}) collective-permute-start(bf16[2,256,256]{1,2,0:T(8,128)(2,1)S(1)} %collective-permute-done.3), channel_id=1, source_target_pairs={{0,4},{4,8},{8,12},{12,16},{16,20},{20,24},{24,28},{28,32},{32,36}... | collective-permute-start | bytes 786440 | tf_op jit(solution)/shard_map/ppermute | solution.py:12
  55.3 0.6 fusion.93
  55.9 8.5 %collective-permute-done.4 = bf16[2,256,256]{1,2,0:T(8,128)(2,1)S(1)} collective-permute-done((bf16[2,256,256]{1,2,0:T(8,128)(2,1)S(1)}, bf16[2,256,256]{1,2,0:T(8,128)(2,1)S(1)}, u32[]{:S(2)}, u32[]{:S(2)}) %collective-permute-start.4) | collective-permute-done | bytes 262176 | tf_op jit(solution)/shard_map/ppermute | solution.py:12
  64.4 1.9 %collective-permute-start.5 = (bf16[2,256,256]{1,2,0:T(8,128)(2,1)S(1)}, bf16[2,256,256]{1,2,0:T(8,128)(2,1)S(1)}, u32[]{:S(2)}, u32[]{:S(2)}) collective-permute-start(bf16[2,256,256]{1,2,0:T(8,128)(2,1)S(1)} %collective-permute-done.4), channel_id=1, source_target_pairs={{0,4},{4,8},{8,12},{12,16},{16,20},{20,24},{24,28},{28,32},{32,36}... | collective-permute-start | bytes 786440 | tf_op jit(solution)/shard_map/ppermute | solution.py:12
  66.4 0.6 fusion.92
  66.9 8.5 %collective-permute-done.5 = bf16[2,256,256]{1,2,0:T(8,128)(2,1)S(1)} collective-permute-done((bf16[2,256,256]{1,2,0:T(8,128)(2,1)S(1)}, bf16[2,256,256]{1,2,0:T(8,128)(2,1)S(1)}, u32[]{:S(2)}, u32[]{:S(2)}) %collective-permute-start.5) | collective-permute-done | bytes 262176 | tf_op jit(solution)/shard_map/ppermute | solution.py:12
  75.5 1.9 %collective-permute-start.6 = (bf16[2,256,256]{1,2,0:T(8,128)(2,1)S(1)}, bf16[2,256,256]{1,2,0:T(8,128)(2,1)S(1)}, u32[]{:S(2)}, u32[]{:S(2)}) collective-permute-start(bf16[2,256,256]{1,2,0:T(8,128)(2,1)S(1)} %collective-permute-done.5), channel_id=1, source_target_pairs={{0,4},{4,8},{8,12},{12,16},{16,20},{20,24},{24,28},{28,32},{32,36}... | collective-permute-start | bytes 786440 | tf_op jit(solution)/shard_map/ppermute | solution.py:12
  77.4 0.6 fusion.91
  77.9 8.5 %collective-permute-done.6 = bf16[2,256,256]{1,2,0:T(8,128)(2,1)S(1)} collective-permute-done((bf16[2,256,256]{1,2,0:T(8,128)(2,1)S(1)}, bf16[2,256,256]{1,2,0:T(8,128)(2,1)S(1)}, u32[]{:S(2)}, u32[]{:S(2)}) %collective-permute-start.6) | collective-permute-done | bytes 262176 | tf_op jit(solution)/shard_map/ppermute | solution.py:12
  86.5 2.1 %collective-permute-start.7 = (bf16[2,256,256]{1,2,0:T(8,128)(2,1)S(1)}, bf16[2,256,256]{1,2,0:T(8,128)(2,1)S(1)}, u32[]{:S(2)}, u32[]{:S(2)}) collective-permute-start(bf16[2,256,256]{1,2,0:T(8,128)(2,1)S(1)} %collective-permute-done.6), channel_id=1, source_target_pairs={{0,4},{4,8},{8,12},{12,16},{16,20},{20,24},{24,28},{28,32},{32,36}... | collective-permute-start | bytes 786440 | tf_op jit(solution)/shard_map/ppermute | solution.py:12
  88.6 0.6 fusion.90
  89.2 8.3 %collective-permute-done.7 = bf16[2,256,256]{1,2,0:T(8,128)(2,1)S(1)} collective-permute-done((bf16[2,256,256]{1,2,0:T(8,128)(2,1)S(1)}, bf16[2,256,256]{1,2,0:T(8,128)(2,1)S(1)}, u32[]{:S(2)}, u32[]{:S(2)}) %collective-permute-start.7) | collective-permute-done | bytes 262176 | tf_op jit(solution)/shard_map/ppermute | solution.py:12
  97.5 0.6 fusion.89
  98.1 0.3 fusion.16
  98.4 0.3 fusion.14
  98.7 0.3 fusion.12
  99.0 0.3 fusion.10
  99.3 0.3 fusion.8
  99.6 0.3 fusion.6
  99.9 0.3 fusion.4
  100.2 0.3 fusion.2
  100.5 0.3 fusion
  100.8 0.1 bitcast_add_fusion
  100.9 0.5 fusion.19
  101.4 0.5 fusion.35
  102.0 0.5 fusion.33
  102.5 0.5 fusion.31
  103.0 0.5 fusion.29
  103.5 0.0 slice-start
  103.5 0.5 fusion.27
  104.1 0.5 fusion.25
  104.6 0.0 slice-start.1
  104.6 0.5 fusion.23
  105.1 0.5 fusion.36
  105.7 0.1 slice-done
  105.7 1.5 %slice-done.1 = s8[4194304]{0:T(1024)(128)(4,1)S(1)} async-done(((s8[8388608]{0:T(1024)(128)(4,1)}), s8[4194304]{0:T(1024)(128)(4,1)S(1)}, s32[]{:S(2)}) %slice-start.1) | async-done | bytes 4194328
  107.2 3.9 %convolution_convert_fusion = bf16[256,4096]{1,0:T(8,128)(2,1)} fusion(bf16[256,1024]{0,1:T(8,128)(2,1)S(1)} %bitcast.324, bf16[1024,4096]{1,0:T(8,128)(2,1)S(1)} %bitcast.323), kind=kOutput, calls=%fused_computation | convolution fusion | flops 2148532224 | bytes 11010048 | tf_op jit(solution)/shard_map/dot_general | solution.py:77
  111.1 0.0 reduce-scatter.2.cloned.1.call-update
  111.4 1.0 copy.101
  112.4 0.6 log_add_fusion
  113.0 29.6 %reduce-scatter.2.cloned.1.call-done = bf16[64,4096]{1,0:T(8,128)(2,1)} async-done(((bf16[256,4096]{1,0:T(8,128)(2,1)}), bf16[64,4096]{1,0:T(8,128)(2,1)}) %reduce-scatter.2.cloned.1.call-update) | async-done | bytes 524304 | tf_op jit(solution)/shard_map/reduce_scatter | solution.py:76
  (41 shorter events, 0.5 us)
Async XLA Ops:
  7.2 135.4 %reduce-scatter.2.cloned.1.call-start = ((), (), s32[]{:S(2)}) async-start(), calls=%async_computation.1 | async-start | bytes 2621440 | tf_op jit(solution)/shard_map/reduce_scatter | solution.py:76
  9.3 11.0 %collective-permute-start = (bf16[2,256,256]{1,2,0:T(8,128)(2,1)S(1)}, bf16[2,256,256]{1,2,0:T(8,128)(2,1)S(1)}, u32[]{:S(2)}, u32[]{:S(2)}) collective-permute-start(bf16[2,256,256]{1,2,0:T(8,128)(2,1)S(1)} %pad_maximum_fusion), channel_id=1, source_target_pairs={{0,4},{4,8},{8,12},{12,16},{16,20},{20,24},{24,28},{28,32},{32,36}... | collective-permute-start | bytes 786440 | tf_op jit(solution)/shard_map/ppermute | solution.py:12
  20.3 11.0 %collective-permute-start.1 = (bf16[2,256,256]{1,2,0:T(8,128)(2,1)S(1)}, bf16[2,256,256]{1,2,0:T(8,128)(2,1)S(1)}, u32[]{:S(2)}, u32[]{:S(2)}) collective-permute-start(bf16[2,256,256]{1,2,0:T(8,128)(2,1)S(1)} %collective-permute-done), channel_id=1, source_target_pairs={{0,4},{4,8},{8,12},{12,16},{16,20},{20,24},{24,28},{28,32},{32,36}... | collective-permute-start | bytes 786440 | tf_op jit(solution)/shard_map/ppermute | solution.py:12
  31.3 11.0 %collective-permute-start.2 = (bf16[2,256,256]{1,2,0:T(8,128)(2,1)S(1)}, bf16[2,256,256]{1,2,0:T(8,128)(2,1)S(1)}, u32[]{:S(2)}, u32[]{:S(2)}) collective-permute-start(bf16[2,256,256]{1,2,0:T(8,128)(2,1)S(1)} %collective-permute-done.1), channel_id=1, source_target_pairs={{0,4},{4,8},{8,12},{12,16},{16,20},{20,24},{24,28},{28,32},{32,36}... | collective-permute-start | bytes 786440 | tf_op jit(solution)/shard_map/ppermute | solution.py:12
  42.4 11.0 %collective-permute-start.3 = (bf16[2,256,256]{1,2,0:T(8,128)(2,1)S(1)}, bf16[2,256,256]{1,2,0:T(8,128)(2,1)S(1)}, u32[]{:S(2)}, u32[]{:S(2)}) collective-permute-start(bf16[2,256,256]{1,2,0:T(8,128)(2,1)S(1)} %collective-permute-done.2), channel_id=1, source_target_pairs={{0,4},{4,8},{8,12},{12,16},{16,20},{20,24},{24,28},{28,32},{32,36}... | collective-permute-start | bytes 786440 | tf_op jit(solution)/shard_map/ppermute | solution.py:12
  53.4 11.0 %collective-permute-start.4 = (bf16[2,256,256]{1,2,0:T(8,128)(2,1)S(1)}, bf16[2,256,256]{1,2,0:T(8,128)(2,1)S(1)}, u32[]{:S(2)}, u32[]{:S(2)}) collective-permute-start(bf16[2,256,256]{1,2,0:T(8,128)(2,1)S(1)} %collective-permute-done.3), channel_id=1, source_target_pairs={{0,4},{4,8},{8,12},{12,16},{16,20},{20,24},{24,28},{28,32},{32,36}... | collective-permute-start | bytes 786440 | tf_op jit(solution)/shard_map/ppermute | solution.py:12
  64.4 11.0 %collective-permute-start.5 = (bf16[2,256,256]{1,2,0:T(8,128)(2,1)S(1)}, bf16[2,256,256]{1,2,0:T(8,128)(2,1)S(1)}, u32[]{:S(2)}, u32[]{:S(2)}) collective-permute-start(bf16[2,256,256]{1,2,0:T(8,128)(2,1)S(1)} %collective-permute-done.4), channel_id=1, source_target_pairs={{0,4},{4,8},{8,12},{12,16},{16,20},{20,24},{24,28},{28,32},{32,36}... | collective-permute-start | bytes 786440 | tf_op jit(solution)/shard_map/ppermute | solution.py:12
  75.5 11.0 %collective-permute-start.6 = (bf16[2,256,256]{1,2,0:T(8,128)(2,1)S(1)}, bf16[2,256,256]{1,2,0:T(8,128)(2,1)S(1)}, u32[]{:S(2)}, u32[]{:S(2)}) collective-permute-start(bf16[2,256,256]{1,2,0:T(8,128)(2,1)S(1)} %collective-permute-done.5), channel_id=1, source_target_pairs={{0,4},{4,8},{8,12},{12,16},{16,20},{20,24},{24,28},{28,32},{32,36}... | collective-permute-start | bytes 786440 | tf_op jit(solution)/shard_map/ppermute | solution.py:12
  86.5 11.0 %collective-permute-start.7 = (bf16[2,256,256]{1,2,0:T(8,128)(2,1)S(1)}, bf16[2,256,256]{1,2,0:T(8,128)(2,1)S(1)}, u32[]{:S(2)}, u32[]{:S(2)}) collective-permute-start(bf16[2,256,256]{1,2,0:T(8,128)(2,1)S(1)} %collective-permute-done.6), channel_id=1, source_target_pairs={{0,4},{4,8},{8,12},{12,16},{16,20},{20,24},{24,28},{28,32},{32,36}... | collective-permute-start | bytes 786440 | tf_op jit(solution)/shard_map/ppermute | solution.py:12
  103.5 2.2 %slice-start = ((s8[8388608]{0:T(1024)(128)(4,1)}), s8[4194304]{0:T(1024)(128)(4,1)S(1)}, s32[]{:S(2)}) async-start(s8[8388608]{0:T(1024)(128)(4,1)} %bitcast.322), calls=%async_computation.2 | async-start | bytes 8388608
  104.6 2.6 %slice-start.1 = ((s8[8388608]{0:T(1024)(128)(4,1)}), s8[4194304]{0:T(1024)(128)(4,1)S(1)}, s32[]{:S(2)}) async-start(s8[8388608]{0:T(1024)(128)(4,1)} %bitcast.322), calls=%async_computation.3 | async-start | bytes 8388608
Sparse Core Ops, SparseCore 0:
  111.2 31.2 reduce-scatter.1
where the time goes:
time: 152 us; the launch traced here: 149 us
  waiting for transfers between devices  92.7 us (61%)
  starting transfers between devices  15.6 us (10%)
  between operations  14.4 us (9%)
  matrix products  13.5 us (9%)
  local copies, waits for them, and re-layouts  7.98 us (5%)
  other arithmetic  5.26 us (3%)
    ppermute x8, waiting for transfers between devices, from_behind(): return lax.ppermute(block, axis, route)  63.1 us
    reduce_scatter x1, waiting for transfers between devices, local(): lax.psum_scatter(jnp.dot(attended, out_weight, preferred_element_type=jnp...  29.6 us
    ppermute x8, starting transfers between devices, from_behind(): return lax.ppermute(block, axis, route)  15.5 us
    dot_general x9, matrix products, attend(): jnp.einsum('qgrd,kgd->grqk', qheads, kh, preferred_element_type=jnp.float32)  4.92 us
    dot_general x9, matrix products, attend(): jnp.einsum('grqk,kgd->qgrd', expo.astype(jnp.bfloat16), vh, preferred_ele...  4.67 us
    dot_general x1, matrix products, local(): jnp.dot(attended, out_weight, preferred_element_type=jnp.float32)  3.87 us
    unnamed x6, local copies, waits for them, and re-layouts  3.59 us
  transfers between devices with their start and end apart: 9, of which 9 were waited for; matrix products, arithmetic and copies ran while one was open for 7% of the time, Pallas kernels for 0%

commit v1 on v0

v1 whole, which is shorter than its diff:
```python
import jax
import jax.numpy as jnp
from jax import lax
from jax.experimental import pallas as pl
from jax.experimental.pallas import tpu as pltpu
from jax.sharding import PartitionSpec as P

HD = 128
T = 256
NX, NC, NY = 4, 2, 4
ROW = NX * NC
KV, GROUP = 2, 4
HQ = KV * GROUP
DOCS = 16
D = 4096
OWNED = T // NY
COLS = 512
PIECES = D // COLS
HALF = PIECES // 2
FAR = -1e30
MESH = pl.DeviceIdType.MESH
F32, BF16 = jnp.float32, jnp.bfloat16
SCALE = HD**-0.5
LOG2E = 1.4426950408889634


def kernel(
    len_ref, q_hbm, k_hbm, v_hbm, w_hbm,
    att_out, lse_out, proj_out,
    q, kv, w, qaug, kaug, score, top, acc, att, lse, part, far, near, comb, proj,
    q_sem, own_sem, w_sem, out_sem,
    z_send, x_send, sib_send, kv_recv, far_send, far_recv, near_send, near_recv,
):
    ctx, me_y = lax.axis_index("ctx"), lax.axis_index("head")
    depth = lax.axis_size("ctx") // ROW
    z, i8 = ctx // ROW, lax.rem(ctx, ROW)
    x, c = i8 // NC, lax.rem(i8, NC)

    def at_x(d):
        return lax.rem(x + d, NX)

    def dev(zz, xx, cc):
        return (zz * ROW + xx * NC + cc, me_y)

    z_up, z_down = lax.rem(z + 1, depth), lax.rem(z + depth - 1, depth)
    right, left, across = (lax.rem(me_y + d, NY) for d in (1, NY - 1, 2))
    sibling = dev(z, x, 1 - c)

    barrier = pltpu.get_barrier_semaphore()
    peers = [dev(z_up, x, c), dev(z_down, x, c), sibling, (ctx, right), (ctx, left)]
    peers += [dev(z, at_x(d), c) for d in (1, 2, 3)]
    for peer in peers:
        pl.semaphore_signal(barrier, inc=1, device_id=peer, device_id_type=MESH)

    own_src = [k_hbm.at[:, pl.ds(g * HD, HD)] for g in range(KV)]
    own_src += [v_hbm.at[:, pl.ds(g * HD, HD)] for g in range(KV)]
    q_copy = pltpu.make_async_copy(q_hbm, q, q_sem)
    own_copies = [pltpu.make_async_copy(own_src[j], kv.at[ROW, j], own_sem.at[j]) for j in range(2 * KV)]

    def column(i):
        return pl.multiple_of(lax.rem(i, 2) * (D // 2) + (i // 2) * COLS, COLS)

    def w_copy(i):
        return pltpu.make_async_copy(w_hbm.at[:, pl.ds(column(i), COLS)], w.at[i], w_sem.at[i])

    q_copy.start()
    for copy in own_copies:
        copy.start()

    pl.semaphore_wait(barrier, len(peers))

    def remote(src, dst, send, recv, device):
        return pltpu.make_async_remote_copy(
            src_ref=src, dst_ref=dst, send_sem=send, recv_sem=recv, device_id=device, device_id_type=MESH
        )

    def z_copy(j):
        return remote(own_src[j], kv.at[i8, j], z_send.at[j], kv_recv.at[i8, j], dev(z_up, x, c))

    def x_copy(src, d, j):
        return remote(src, kv.at[i8, j], x_send.at[d - 1, j], kv_recv.at[i8, j], dev(z, at_x(d), c))

    def sib_copy(src, slot, d, j):
        return remote(src, kv.at[slot, j], sib_send.at[d, j], kv_recv.at[slot, j], sibling)

    def arrived(slot, j):
        remote(kv.at[slot, j], kv.at[slot, j], z_send.at[j], kv_recv.at[slot, j], sibling).wait_recv()

    for j in range(2 * KV):
        z_copy(j).start()
        for d in (1, 3, 2):
            @pl.when(at_x(d) > x)
            def _():
                x_copy(own_src[j], d, j).start()
        @pl.when(c == 0)
        def _():
            sib_copy(own_src[j], i8, 0, j).start()

    def relay(j):
        arrived(i8, j)
        for d in (1, 3, 2):
            @pl.when(at_x(d) < x)
            def _():
                x_copy(kv.at[i8, j], d, j).start()
        @pl.when(c == 1)
        def _():
            sib_copy(kv.at[i8, j], i8, 0, j).start()

    def forward(j):
        for d in (1, 3, 2):
            slot = at_x(d) * NC + c
            arrived(slot, j)
            sib_copy(kv.at[slot, j], slot, d, j).start()

    def from_sibling(j):
        for d in (1, 3, 2):
            arrived(at_x(d) * NC + 1 - c, j)

    def w_start(i, carry):
        w_copy(i).start()
        return carry

    lax.fori_loop(0, PIECES, w_start, 0)

    lane = lax.broadcasted_iota(jnp.int32, (1, HD), 1)
    first = jnp.zeros((1, HD), jnp.int32)
    last = jnp.zeros((1, HD), jnp.int32)
    end = jnp.int32(0)
    for d in range(DOCS):
        first = jnp.where(lane == d, end, first)
        end = end + len_ref[d]
        last = jnp.where(lane == d, end, last)
    token = lax.broadcasted_iota(jnp.int32, (T, HD), 0)

    def inside(block):
        position = block * T + token
        return (position >= first) & (position < last)

    qaug[...] = jnp.where(inside(ctx), 1.0, 0.0).astype(BF16)

    def slot_of(n):
        d = lax.rem(n, 3) + 1
        row = lax.rem(x + d, NX) * NC
        slot = jnp.where(n < 6, row + c, row + 1 - c)
        slot = jnp.where(n == 0, ROW, slot)
        slot = jnp.where(n == 1, i8, slot)
        return jnp.where(n == 2, x * NC + 1 - c, slot)

    def block_of(n):
        slot = slot_of(n)
        block = jnp.where(slot < i8, z * ROW + slot, (z - 1) * ROW + slot)
        return jnp.where(n == 0, ctx, block)

    def build(n, carry):
        kaug[n] = jnp.where(inside(block_of(n)), 0.0, FAR).astype(BF16)
        return carry

    lax.fori_loop(0, ROW + 1, build, 0)

    def scores(n, g, own):
        slot = slot_of(n)
        keys = jnp.concatenate([kv[slot, g], kaug[n]], axis=1)

        def head(r, carry):
            h = g * GROUP + r
            cols = pl.ds(pl.multiple_of(h * HD, HD), HD)
            queries = jnp.concatenate([q[:, cols], qaug[...]], axis=1)
            s = lax.dot_general(queries, keys, (((1,), (1,)), ((), ())), preferred_element_type=F32)
            if own:
                row = lax.broadcasted_iota(jnp.int32, (T, T), 0)
                col = lax.broadcasted_iota(jnp.int32, (T, T), 1)
                s = jnp.where(col <= row, s, FAR)
            score[n, h] = s
            high = jnp.maximum(s[:, :HD], s[:, HD:])
            top[h] = high if own else jnp.maximum(top[h], high)
            return carry

        lax.fori_loop(0, GROUP, head, 0)

    def scores_of(lo, hi, g):
        def body(n, carry):
            scores(n, g, False)
            return carry

        lax.fori_loop(lo, hi, body, 0)

    relay(0)
    q_copy.wait()
    for copy in own_copies:
        copy.wait()
    scores(0, 0, True)
    relay(1)
    scores(0, 1, True)
    for g in range(KV):
        arrived(x * NC + 1 - c, g)
        scores_of(1, 3, g)
    forward(0)
    relay(2)
    scores_of(3, 6, 0)
    forward(1)
    relay(3)
    scores_of(3, 6, 1)
    for g in range(KV):
        from_sibling(g)
        scores_of(6, 9, g)

    def spread(h, carry):
        top[h] = jnp.broadcast_to(jnp.max(top[h], axis=1, keepdims=True), (T, HD))
        return carry

    lax.fori_loop(0, HQ, spread, 0)

    ones = jnp.ones((3 * T, HD), BF16)

    def mix(group, g):
        values = [kv[slot_of(group * 3 + i), KV + g] for i in range(3)]
        values = jnp.concatenate([jnp.concatenate(values, axis=0), ones], axis=1)

        def head(r, carry):
            h = g * GROUP + r
            high = top[h]
            high = jnp.concatenate([high, high], axis=1)
            weight = [
                jnp.exp2((score[group * 3 + i, h] - high) * (SCALE * LOG2E)).astype(BF16) for i in range(3)
            ]
            mixed = jnp.dot(jnp.concatenate(weight, axis=1), values, preferred_element_type=F32)
            acc[h] = mixed if group == 0 else acc[h] + mixed
            return carry

        lax.fori_loop(0, GROUP, head, 0)

    for g in range(KV):
        arrived(x * NC + 1 - c, KV + g)
        mix(0, g)
    for g in range(KV):
        forward(KV + g)
        mix(1, g)
    for g in range(KV):
        from_sibling(KV + g)
        mix(2, g)

    def finish(h, carry):
        total = acc[h, :, HD:]
        cols = pl.ds(pl.multiple_of(h * HD, HD), HD)
        att[:, cols] = (acc[h, :, :HD] / total).astype(BF16)
        return jnp.where(lane == h, top[h] * SCALE + jnp.log(total), carry)

    sums = lax.fori_loop(0, HQ, finish, jnp.zeros((T, HD), F32))
    lse[...] = sums.T[:HQ]
    att_copy = pltpu.make_async_copy(att, att_out, out_sem.at[0])
    lse_copy = pltpu.make_async_copy(lse, lse_out, out_sem.at[1])

    def rows(y):
        return pl.ds(pl.multiple_of(y * OWNED, OWNED), OWNED)

    def far_copy(i):
        side = lax.rem(i, 2)
        target = jnp.where(side == 0, right, left)
        return remote(part.at[rows(across), pl.ds(column(i), COLS)], far.at[i], far_send.at[i], far_recv.at[i], (ctx, target))

    def near_copy(i):
        side = lax.rem(i, 2)
        target = jnp.where(side == 0, left, right)
        return remote(
            part.at[rows(target), pl.ds(column(i), COLS)], near.at[1 - side, i],
            near_send.at[0, i], near_recv.at[1 - side, i], (ctx, target),
        )

    def comb_copy(i):
        side = lax.rem(i, 2)
        target = jnp.where(side == 0, right, left)
        return remote(comb.at[i], near.at[side, i], near_send.at[1, i], near_recv.at[side, i], (ctx, target))

    def project(i, carry):
        w_copy(i).wait()
        part[:, pl.ds(column(i), COLS)] = jnp.dot(att[...], w[i], preferred_element_type=F32).astype(BF16)
        far_copy(i).start()
        return carry

    lax.fori_loop(0, PIECES, project, 0)
    att_copy.start()
    lse_copy.start()

    def send_near(i, carry):
        near_copy(i).start()
        return carry

    lax.fori_loop(0, PIECES, send_near, 0)

    def combine(i, carry):
        target = jnp.where(lax.rem(i, 2) == 0, right, left)
        far_copy(i).wait_recv()
        mine = part[rows(target), pl.ds(column(i), COLS)].astype(F32)
        comb[i] = (mine + far[i].astype(F32)).astype(BF16)
        comb_copy(i).start()
        return carry

    lax.fori_loop(0, PIECES, combine, 0)

    def proj_copy(i):
        return pltpu.make_async_copy(proj.at[i], proj_out.at[:, pl.ds(column(i), COLS)], out_sem.at[2 + i])

    def total(i, carry):
        near_copy(i).wait_recv()
        comb_copy(i).wait_recv()
        mine = part[rows(me_y), pl.ds(column(i), COLS)].astype(F32)
        proj[i] = (mine + near[0, i].astype(F32) + near[1, i].astype(F32)).astype(BF16)
        proj_copy(i).start()
        return carry

    lax.fori_loop(0, PIECES, total, 0)

    for j in range(2 * KV):
        z_copy(j).wait_send()
        for d in (1, 2, 3):
            x_copy(kv.at[i8, j], d, j).wait_send()
            sib_copy(kv.at[i8, j], i8, d, j).wait_send()
        sib_copy(kv.at[i8, j], i8, 0, j).wait_send()

    def drain(i, carry):
        far_copy(i).wait_send()
        near_copy(i).wait_send()
        comb_copy(i).wait_send()
        proj_copy(i).wait()
        return carry

    lax.fori_loop(0, PIECES, drain, 0)
    att_copy.wait()
    lse_copy.wait()


def local(queries, keys, values, lengths, out_weight):
    hbm = pl.BlockSpec(memory_space=pl.ANY)
    dma = pltpu.SemaphoreType.DMA
    return pl.pallas_call(
        kernel,
        out_shape=(
            jax.ShapeDtypeStruct((T, HQ * HD), BF16),
            jax.ShapeDtypeStruct((HQ, T), F32),
            jax.ShapeDtypeStruct((OWNED, D), BF16),
        ),
        in_specs=[pl.BlockSpec(memory_space=pltpu.SMEM)] + [hbm] * 4,
        out_specs=(hbm,) * 3,
        scratch_shapes=[
            pltpu.VMEM((T, HQ * HD), BF16),
            pltpu.VMEM((ROW + 1, 2 * KV, T, HD), BF16),
            pltpu.VMEM((PIECES, HQ * HD, COLS), BF16),
            pltpu.VMEM((T, HD), BF16),
            pltpu.VMEM((ROW + 1, T, HD), BF16),
            pltpu.VMEM((ROW + 1, HQ, T, T), F32),
            pltpu.VMEM((HQ, T, HD), F32),
            pltpu.VMEM((HQ, T, 2 * HD), F32),
            pltpu.VMEM((T, HQ * HD), BF16),
            pltpu.VMEM((HQ, T), F32),
            pltpu.VMEM((T, D), BF16),
            pltpu.VMEM((PIECES, OWNED, COLS), BF16),
            pltpu.VMEM((2, PIECES, OWNED, COLS), BF16),
            pltpu.VMEM((PIECES, OWNED, COLS), BF16),
            pltpu.VMEM((PIECES, OWNED, COLS), BF16),
            dma, dma((2 * KV,)), dma((PIECES,)), dma((2 + PIECES,)),
            dma((2 * KV,)), dma((3, 2 * KV)), dma((4, 2 * KV)), dma((ROW, 2 * KV)),
            dma((PIECES,)), dma((PIECES,)), dma((2, PIECES)), dma((2, PIECES)),
        ],
        compiler_params=pltpu.CompilerParams(
            collective_id=0, has_side_effects=True, vmem_limit_bytes=56 * 2**20
        ),
    )(lengths, queries, keys, values, out_weight)


def solution(mesh):
    placed = (P("ctx", "head"), P("ctx", "head"), P("ctx", "head"), P(), P("head", None))
    return jax.shard_map(
        local,
        mesh=mesh,
        in_specs=placed,
        out_specs=(P("ctx", "head"), P("head", "ctx"), P(("ctx", "head"), None)),
        check_vma=False,
    )
```

time: 152 us -> 66.3 us (0.44)
  the two profiles are of different devices: /device:TPU:128 before, /device:TPU:1 now
where the time goes in v1:
time: 66.3 us; the launch traced here: 66.1 us
  Pallas kernels  60.4 us (91%)
  local copies, waits for them, and re-layouts  5.03 us (8%)
    pallas_call x1, Pallas kernels, local(): pl.pallas_call(kernel, out_shape=(jax.ShapeDtypeStruct((T, HQ * HD), BF16...  60.4 us
    unnamed x3, local copies, waits for them, and re-layouts  5.03 us

profile of v1, /device:TPU:1, one launch (start us, length us, event | category | flops | bytes accessed | tf_op | source)
XLA Modules:
  0.0 66.1 jit_solution(16001392130902198042)
XLA Ops:
  0.6 60.4 %shard_map.76 = (bf16[256,1024]{1,0:T(8,128)(2,1)}, f32[8,256]{1,0:T(8,128)}, bf16[64,4096]{1,0:T(8,128)(2,1)}) custom-call(s32[16]{0:T(128)} %len_ref.1, bf16[256,1024]{1,0:T(8,128)(2,1)} %q_hbm.1, bf16[256,256]{1,0:T(8,128)(2,1)} %k_hbm.1, bf16[256,256]{1,0:T(8,128)(2,1)} %v_hbm.1, bf16[1024,4096]{1,0:T(8,128)(2,1)} %w_hbm.1), custom_call_target="tpu_custom_call" | custom-call | tf_op jit(solution)/shard_map/pallas_call | solution.py:335
  61.1 1.9 %copy.11 = bf16[256,1024]{1,0:T(8,128)(2,1)} copy(bf16[256,1024]{1,0:T(8,128)(2,1)} %get-tuple-element.6) | data formatting | bytes 1048576
  63.0 1.3 %copy.12 = f32[8,256]{1,0:T(8,128)} copy(f32[8,256]{1,0:T(8,128)} %get-tuple-element.7) | data formatting | bytes 16384
  64.2 1.9 %copy.13 = bf16[64,4096]{1,0:T(8,128)(2,1)} copy(bf16[64,4096]{1,0:T(8,128)(2,1)} %get-tuple-element.8) | data formatting | bytes 1048576

commit v2 on v1

v2 whole, which is shorter than its diff:
```python
import jax
import jax.numpy as jnp
from jax import lax
from jax.experimental import pallas as pl
from jax.experimental.pallas import tpu as pltpu
from jax.sharding import PartitionSpec as P

HD = 128
T = 256
NX, NC, NY = 4, 2, 4
ROW = NX * NC
KV, GROUP = 2, 4
HQ = KV * GROUP
DOCS = 16
D = 4096
OWNED = T // NY
COLS = 512
PIECES = D // COLS
HALF = PIECES // 2
FAR = -1e30
MESH = pl.DeviceIdType.MESH
F32, BF16 = jnp.float32, jnp.bfloat16
SCALE = HD**-0.5
LOG2E = 1.4426950408889634


def kernel(
    len_ref, q_hbm, k_hbm, v_hbm, w_hbm,
    att, lse, proj,
    q, kv, passing, w, qaug, kaug, score, top, acc, part, far, near, comb,
    q_sem, own_sem, w_sem,
    z_send, x_send, sib_send, kv_recv, pass_recv, far_send, far_recv, near_send, near_recv,
):
    ctx, me_y = lax.axis_index("ctx"), lax.axis_index("head")
    depth = lax.axis_size("ctx") // ROW
    z, i8 = ctx // ROW, lax.rem(ctx, ROW)
    x, c = i8 // NC, lax.rem(i8, NC)

    def head_columns(h):
        return pl.ds(pl.multiple_of(h * HD, HD), HD)

    def at_x(d):
        return lax.rem(x + d, NX)

    def dev(zz, xx, cc):
        return (zz * ROW + xx * NC + cc, me_y)

    z_up, z_down = lax.rem(z + 1, depth), lax.rem(z + depth - 1, depth)
    right, left, across = (lax.rem(me_y + d, NY) for d in (1, NY - 1, 2))
    sibling = dev(z, x, 1 - c)

    barrier = pltpu.get_barrier_semaphore()
    peers = [dev(z_up, x, c), dev(z_down, x, c), sibling, (ctx, right), (ctx, left)]
    x_up, x_down = dev(z, at_x(1), c), dev(z, at_x(NX - 1), c)
    peers += [x_up, x_down]
    for peer in peers:
        pl.semaphore_signal(barrier, inc=1, device_id=peer, device_id_type=MESH)

    own_src = [k_hbm.at[:, pl.ds(g * HD, HD)] for g in range(KV)]
    own_src += [v_hbm.at[:, pl.ds(g * HD, HD)] for g in range(KV)]
    q_copy = pltpu.make_async_copy(q_hbm, q, q_sem)
    own_copies = [pltpu.make_async_copy(own_src[j], kv.at[ROW, j], own_sem.at[j]) for j in range(2 * KV)]

    def column(i):
        return pl.multiple_of(lax.rem(i, 2) * (D // 2) + (i // 2) * COLS, COLS)

    def w_copy(i):
        return pltpu.make_async_copy(w_hbm.at[:, pl.ds(column(i), COLS)], w.at[i], w_sem.at[i])

    q_copy.start()
    for copy in own_copies:
        copy.start()

    pl.semaphore_wait(barrier, len(peers))

    def remote(src, dst, send, recv, device):
        return pltpu.make_async_remote_copy(
            src_ref=src, dst_ref=dst, send_sem=send, recv_sem=recv, device_id=device, device_id_type=MESH
        )

    slots = [origin * NC + c for origin in range(NX)]

    def sib_copy(src, origin, j):
        slot = origin * NC + c
        return remote(src, kv.at[slot, j], sib_send.at[origin, j], kv_recv.at[slot, j], sibling)

    def arrived(slot, j):
        remote(kv.at[slot, j], kv.at[slot, j], z_send.at[0, j], kv_recv.at[slot, j], sibling).wait_recv()

    started = [[] for _ in range(NX)]
    OWN, PREV, RELAY = range(3)
    UP, DOWN = range(2)

    def send(role, copy, *sem):
        copy.start()
        started[role].append(sem)

    def along_x(role, way, kind, src, dst, recv, j):
        target = x_up if way == UP else x_down
        send(role, remote(src, dst, x_send.at[way, kind, j], recv, target), x_send, way, kind, j)

    def block_along_x(role, way, kind, origin, src, j):
        slot = slots[origin]
        along_x(role, way, kind, src, kv.at[slot, j], kv_recv.at[slot, j], j)

    def to_sibling(role, origin, src, j):
        send(role, sib_copy(src, origin, j), sib_send, origin, j)

    def up_z(role, kind, origin, src, j):
        slot = slots[origin]
        send(role, remote(src, kv.at[slot, j], z_send.at[kind, j], kv_recv.at[slot, j], dev(z_up, x, c)), z_send, kind, j)

    def got(role, origin, j, *ways):
        src = kv.at[slots[origin], j]
        arrived(slots[origin], j)
        for way in ways:
            block_along_x(role, way, RELAY, origin, src, j)
        to_sibling(role, origin, src, j)

    def got_prev(role, j, *ways):
        src = kv.at[slots[role], j]
        arrived(slots[role], j)
        for way in ways:
            block_along_x(role, way, PREV, role, src, j)

        @pl.when(c == 1)
        def _():
            sib_copy(src, role, j).start()

    def pass_on(role, which, origin, j):
        remote(passing.at[which, j // 2], passing.at[which, j // 2], z_send.at[0, j], pass_recv.at[which, j // 2], sibling).wait_recv()
        if which == 0:
            block_along_x(role, DOWN, RELAY, origin, passing.at[which, j // 2], j)
        else:
            up_z(role, 1, origin, passing.at[which, j // 2], j)

    def to_pass(role, way, kind, which, src, j):
        along_x(role, way, kind, src, passing.at[which, j // 2], pass_recv.at[which, j // 2], j)

    def own_sends(role, b):
        for j in (b, b + 1):
            src = own_src[j]
            up_z(role, 0, role, src, j)
            if role == 1 and j == b:
                to_pass(role, DOWN, OWN, 0, src, j)
            if role < 3:
                block_along_x(role, UP, OWN, role, src, j)
            if role == 0:
                block_along_x(role, DOWN, OWN, role, src, j)

            @pl.when(c == 0)
            def _():
                sib_copy(src, role, j).start()

    def stage_1(role, b):
        if role == 0:
            pass_on(0, 0, 1, b)
            got_prev(0, b)
        elif role == 1:
            got(1, 0, b, UP)
            got_prev(1, b, DOWN)
        elif role == 2:
            got_prev(2, b, DOWN)
            got(2, 1, b)
        else:
            arrived(slots[2], b)
            to_pass(3, UP, RELAY, 1, kv.at[slots[2], b], b)
            to_sibling(3, 2, kv.at[slots[2], b], b)
            got_prev(3, b, UP, DOWN)
            got(3, 0, b)

    def stage_2(role, b):
        if role == 0:
            pass_on(0, 1, 2, b)
            got_prev(0, b + 1)
        elif role == 1:
            got_prev(1, b + 1, DOWN)
            got(1, 0, b + 1)
        elif role == 2:
            got_prev(2, b + 1, DOWN)
            got(2, 1, b + 1, UP)
        else:
            got_prev(3, b + 1, UP, DOWN)
            got(3, 0, b + 1, DOWN)
            got(3, 2, b + 1)

    def stage_3(role, b):
        if role == 0:
            got(0, 3, b, UP)
            got(0, 1, b)
            got(0, 1, b + 1)
            got(0, 2, b)
        elif role == 1:
            got(1, 2, b)
            got(1, 2, b + 1, DOWN)
        elif role == 2:
            got(2, 3, b)
            got(2, 3, b + 1, DOWN)
            got(2, 0, b)
        else:
            got(3, 1, b)
            got(3, 1, b + 1)

    def stage_4(role, b):
        if role == 0:
            got(0, 3, b + 1)
            got(0, 2, b + 1)
        elif role == 1:
            got(1, 3, b)
            got(1, 3, b + 1)
        elif role == 2:
            got(2, 0, b + 1)

    def in_role(stage, b):
        for role in range(NX):
            @pl.when(x == role)
            def _():
                stage(role, b)

    in_role(own_sends, 0)

    def from_sibling(j):
        for d in (1, 3, 2):
            arrived(at_x(d) * NC + 1 - c, j)

    def w_start(i, carry):
        w_copy(i).start()
        return carry

    lax.fori_loop(0, PIECES, w_start, 0)

    lane = lax.broadcasted_iota(jnp.int32, (1, HD), 1)
    first = jnp.zeros((1, HD), jnp.int32)
    last = jnp.zeros((1, HD), jnp.int32)
    end = jnp.int32(0)
    for d in range(DOCS):
        first = jnp.where(lane == d, end, first)
        end = end + len_ref[d]
        last = jnp.where(lane == d, end, last)
    token = lax.broadcasted_iota(jnp.int32, (T, HD), 0)

    def inside(block):
        position = block * T + token
        return (position >= first) & (position < last)

    qaug[...] = jnp.where(inside(ctx), 1.0, 0.0).astype(BF16)

    same_slots = [at_x(d) * NC + c for d in (1, 2, 3)]
    other_slots = [at_x(d) * NC + 1 - c for d in (1, 2, 3)]
    block_slots = [ROW + 0 * x, i8, x * NC + 1 - c] + same_slots + other_slots

    def slot_of(n):
        return block_slots[n]

    for n in range(ROW + 1):
        slot = slot_of(n)
        block = jnp.where(slot < i8, z * ROW + slot, (z - 1) * ROW + slot)
        kaug[n] = jnp.where(inside(ctx if n == 0 else block), 0.0, FAR).astype(BF16)

    def scores(first_n, last_n, g):
        for n in range(first_n, last_n):
            keys = jnp.concatenate([kv[slot_of(n), g], kaug[n]], axis=1)
            for r in range(GROUP):
                h = g * GROUP + r
                queries = jnp.concatenate([q[:, head_columns(h)], qaug[...]], axis=1)
                s = lax.dot_general(queries, keys, (((1,), (1,)), ((), ())), preferred_element_type=F32)
                if n == 0:
                    row = lax.broadcasted_iota(jnp.int32, (T, T), 0)
                    col = lax.broadcasted_iota(jnp.int32, (T, T), 1)
                    s = jnp.where(col <= row, s, FAR)
                score[n, h] = s
                high = jnp.maximum(s[:, :HD], s[:, HD:])
                top[h] = high if n == 0 else jnp.maximum(top[h], high)

    def mix(first_n, g):
        values = [kv[slot_of(first_n + i), KV + g] for i in range(3)]
        values = jnp.concatenate([jnp.concatenate(values, axis=0), jnp.ones((3 * T, HD), BF16)], axis=1)
        for r in range(GROUP):
            h = g * GROUP + r
            high = jnp.concatenate([top[h], top[h]], axis=1)
            weight = [jnp.exp2((score[first_n + i, h] - high) * (SCALE * LOG2E)).astype(BF16) for i in range(3)]
            mixed = jnp.dot(jnp.concatenate(weight, axis=1), values, preferred_element_type=F32)
            acc[h] = mixed if first_n == 0 else acc[h] + mixed

    q_copy.wait()
    for copy in own_copies:
        copy.wait()

    def own_scores(g, carry):
        scores(0, 1, g)
        return carry

    def close_scores(g, carry):
        arrived(x * NC + 1 - c, g)
        scores(1, 3, g)
        return carry

    def same_scores(g, carry):
        scores(3, 6, g)
        return carry

    def other_scores(g, carry):
        from_sibling(g)
        scores(6, 9, g)
        return carry

    def close_mix(g, carry):
        arrived(x * NC + 1 - c, KV + g)
        mix(0, g)
        return carry

    def same_mix(g, carry):
        mix(3, g)
        return carry

    def other_mix(g, carry):
        from_sibling(KV + g)
        mix(6, g)
        return carry

    def each_kv(step):
        lax.fori_loop(0, KV, step, 0)

    each_kv(own_scores)
    in_role(stage_1, 0)
    in_role(own_sends, KV)
    in_role(stage_2, 0)
    each_kv(close_scores)
    in_role(stage_3, 0)
    in_role(stage_1, KV)
    in_role(stage_4, 0)
    in_role(stage_2, KV)
    each_kv(same_scores)
    each_kv(other_scores)
    for h in range(HQ):
        top[h] = jnp.broadcast_to(jnp.max(top[h], axis=1, keepdims=True), (T, HD))
    in_role(stage_3, KV)
    each_kv(close_mix)
    in_role(stage_4, KV)
    each_kv(same_mix)
    each_kv(other_mix)

    sums = jnp.zeros((T, HD), F32)
    for h in range(HQ):
        total = acc[h, :, HD:]
        att[:, h * HD : (h + 1) * HD] = (acc[h, :, :HD] / total).astype(BF16)
        sums = jnp.where(lane == h, top[h] * SCALE + jnp.log(total), sums)
    lse[...] = sums.T[:HQ]

    def rows(y):
        return pl.ds(pl.multiple_of(y * OWNED, OWNED), OWNED)

    def far_copy(i):
        side = lax.rem(i, 2)
        target = jnp.where(side == 0, right, left)
        return remote(part.at[rows(across), pl.ds(column(i), COLS)], far.at[i], far_send.at[i], far_recv.at[i], (ctx, target))

    def near_copy(i):
        side = lax.rem(i, 2)
        target = jnp.where(side == 0, left, right)
        return remote(
            part.at[rows(target), pl.ds(column(i), COLS)], near.at[1 - side, i],
            near_send.at[0, i], near_recv.at[1 - side, i], (ctx, target),
        )

    def comb_copy(i):
        side = lax.rem(i, 2)
        target = jnp.where(side == 0, right, left)
        return remote(comb.at[i], near.at[side, i], near_send.at[1, i], near_recv.at[side, i], (ctx, target))

    def project(i, carry):
        w_copy(i).wait()
        part[:, pl.ds(column(i), COLS)] = jnp.dot(att[...], w[i], preferred_element_type=F32).astype(BF16)
        far_copy(i).start()
        return carry

    lax.fori_loop(0, PIECES, project, 0)

    def send_near(i, carry):
        near_copy(i).start()
        return carry

    lax.fori_loop(0, PIECES, send_near, 0)

    def combine(i, carry):
        target = jnp.where(lax.rem(i, 2) == 0, right, left)
        far_copy(i).wait_recv()
        mine = part[rows(target), pl.ds(column(i), COLS)].astype(F32)
        comb[i] = (mine + far[i].astype(F32)).astype(BF16)
        comb_copy(i).start()
        return carry

    lax.fori_loop(0, PIECES, combine, 0)

    def add_up(i, carry):
        near_copy(i).wait_recv()
        comb_copy(i).wait_recv()
        mine = part[rows(me_y), pl.ds(column(i), COLS)].astype(F32)
        proj[:, pl.ds(column(i), COLS)] = (mine + near[0, i].astype(F32) + near[1, i].astype(F32)).astype(BF16)
        return carry

    lax.fori_loop(0, PIECES, add_up, 0)

    for role in range(NX):
        @pl.when(x == role)
        def _():
            for sems, *index in started[role]:
                remote(kv.at[ROW, 0], kv.at[ROW, 0], sems.at[*index], kv_recv.at[0, 0], sibling).wait_send()

    for j in range(2 * KV):
        sib_copy(kv.at[i8, j], x, j).wait_send()

    def drain(i, carry):
        far_copy(i).wait_send()
        near_copy(i).wait_send()
        comb_copy(i).wait_send()
        return carry

    lax.fori_loop(0, PIECES, drain, 0)


def hand_over(*refs):
    sources, targets, sems = refs[:3], refs[3:6], refs[6]
    copies = [pltpu.make_async_copy(a, b, sems.at[i]) for i, (a, b) in enumerate(zip(sources, targets))]
    for copy in copies:
        copy.start()
    for copy in copies:
        copy.wait()


def local(queries, keys, values, lengths, out_weight):
    hbm = pl.BlockSpec(memory_space=pl.ANY)
    dma = pltpu.SemaphoreType.DMA
    results = pl.pallas_call(
        kernel,
        out_shape=(
            pltpu.VMEM((T, HQ * HD), BF16),
            pltpu.VMEM((HQ, T), F32),
            pltpu.VMEM((OWNED, D), BF16),
        ),
        in_specs=[pl.BlockSpec(memory_space=pltpu.SMEM)] + [hbm] * 4,
        out_specs=(pl.BlockSpec(memory_space=pltpu.VMEM),) * 3,
        scratch_shapes=[
            pltpu.VMEM((T, HQ * HD), BF16),
            pltpu.VMEM((ROW + 1, 2 * KV, T, HD), BF16),
            pltpu.VMEM((2, KV, T, HD), BF16),
            pltpu.VMEM((PIECES, HQ * HD, COLS), BF16),
            pltpu.VMEM((T, HD), BF16),
            pltpu.VMEM((ROW + 1, T, HD), BF16),
            pltpu.VMEM((ROW + 1, HQ, T, T), F32),
            pltpu.VMEM((HQ, T, HD), F32),
            pltpu.VMEM((HQ, T, 2 * HD), F32),
            pltpu.VMEM((T, D), BF16),
            pltpu.VMEM((PIECES, OWNED, COLS), BF16),
            pltpu.VMEM((2, PIECES, OWNED, COLS), BF16),
            pltpu.VMEM((PIECES, OWNED, COLS), BF16),
            dma, dma((2 * KV,)), dma((PIECES,)),
            dma((2, 2 * KV)), dma((2, 3, 2 * KV)), dma((NX, 2 * KV)), dma((ROW, 2 * KV)), dma((2, KV)),
            dma((PIECES,)), dma((PIECES,)), dma((2, PIECES)), dma((2, PIECES)),
        ],
        compiler_params=pltpu.CompilerParams(
            collective_id=0, has_side_effects=True, vmem_limit_bytes=56 * 2**20
        ),
    )(lengths, queries, keys, values, out_weight)
    results = [pltpu.with_memory_space_constraint(r, pltpu.VMEM) for r in results]
    return pl.pallas_call(
        hand_over,
        out_shape=tuple(jax.ShapeDtypeStruct(r.shape, r.dtype) for r in results),
        in_specs=[pl.BlockSpec(memory_space=pltpu.VMEM)] * 3,
        out_specs=(hbm,) * 3,
        scratch_shapes=[dma((3,))],
    )(*results)


def solution(mesh):
    placed = (P("ctx", "head"), P("ctx", "head"), P("ctx", "head"), P(), P("head", None))
    return jax.shard_map(
        local,
        mesh=mesh,
        in_specs=placed,
        out_specs=(P("ctx", "head"), P("head", "ctx"), P(("ctx", "head"), None)),
        check_vma=False,
    )
```

time: 66.3 us -> 53.3 us (0.80)
  the two profiles are of different devices: /device:TPU:1 before, /device:TPU:2 now
where the time goes in v2:
time: 53.3 us; the launch traced here: 53.2 us
  Pallas kernels  52.6 us (99%)
  between operations  0.64 us (1%)
    pallas_call x1, Pallas kernels, local(): pl.pallas_call(kernel, out_shape=(pltpu.VMEM((T, HQ * HD), BF16), pltpu.V...  51.6 us

profile of v2, /device:TPU:2, one launch (start us, length us, event | category | flops | bytes accessed | tf_op | source)
XLA Modules:
  0.0 53.2 jit_solution(13801601128372220663)
XLA Ops:
  0.6 51.6 %shard_map.76 = (bf16[256,1024]{1,0:T(8,128)(2,1)S(1)}, f32[8,256]{1,0:T(8,128)S(1)}, bf16[64,4096]{1,0:T(8,128)(2,1)S(1)}) custom-call(s32[16]{0:T(128)} %len_ref.1, bf16[256,1024]{1,0:T(8,128)(2,1)} %q_hbm.1, bf16[256,256]{1,0:T(8,128)(2,1)} %k_hbm.1, bf16[256,256]{1,0:T(8,128)(2,1)} %v_hbm.1, bf16[1024,4096]{1,0:T(8,128)(2,1)} %w_hbm.1), custom_call_target="tpu_custom_call" | custom-call | tf_op jit(solution)/shard_map/pallas_call | solution.py:434
  52.2 1.0 %shard_map.77 = (bf16[256,1024]{1,0:T(8,128)(2,1)}, f32[8,256]{1,0:T(8,128)}, bf16[64,4096]{1,0:T(8,128)(2,1)}) custom-call(bf16[256,1024]{1,0:T(8,128)(2,1)S(1)} %get-tuple-element.6.refs_0_, f32[8,256]{1,0:T(8,128)S(1)} %get-tuple-element.7.refs_1_, bf16[64,4096]{1,0:T(8,128)(2,1)S(1)} %get-tuple-element.8.refs_2_), custom_call_target="tpu_custom_call" | custom-call | tf_op jit(solution)/shard_map/pallas_call | solution.py:466

commit v3 on v2

--- a/solution.py
+++ b/solution.py
@@ -1,3 +1,5 @@
+import functools
+
 import jax
 import jax.numpy as jnp
 from jax import lax
@@ -27,9 +29,9 @@
 def kernel(
     len_ref, q_hbm, k_hbm, v_hbm, w_hbm,
     att, lse, proj,
-    q, kv, passing, w, qaug, kaug, score, top, acc, part, far, near, comb,
+    q, kv, w, qaug, kaug, score, top, acc, part, far, near, comb,
     q_sem, own_sem, w_sem,
-    z_send, x_send, sib_send, kv_recv, pass_recv, far_send, far_recv, near_send, near_recv,
+    z_send, x_send, sib_send, kv_recv, far_send, far_recv, near_send, near_recv,
 ):
     ctx, me_y = lax.axis_index("ctx"), lax.axis_index("head")
     depth = lax.axis_size("ctx") // ROW
@@ -37,7 +39,7 @@
     x, c = i8 // NC, lax.rem(i8, NC)
 
     def head_columns(h):
-        return pl.ds(pl.multiple_of(h * HD, HD), HD)
+        return pl.ds(h * HD if isinstance(h, int) else pl.multiple_of(h * HD, HD), HD)
 
     def at_x(d):
         return lax.rem(x + d, NX)
@@ -49,12 +51,20 @@
     right, left, across = (lax.rem(me_y + d, NY) for d in (1, NY - 1, 2))
     sibling = dev(z, x, 1 - c)
 
+    has_prev, has_next = z > 0, z < depth - 1
+    x_up, x_down, x_across = (dev(z, at_x(d), c) for d in (1, NX - 1, 2))
+
     barrier = pltpu.get_barrier_semaphore()
-    peers = [dev(z_up, x, c), dev(z_down, x, c), sibling, (ctx, right), (ctx, left)]
-    x_up, x_down = dev(z, at_x(1), c), dev(z, at_x(NX - 1), c)
-    peers += [x_up, x_down]
-    for peer in peers:
+
+    def greet(peer):
         pl.semaphore_signal(barrier, inc=1, device_id=peer, device_id_type=MESH)
+
+    for peer in (x_up, x_down, x_across, sibling, (ctx, right), (ctx, left)):
+        greet(peer)
+    others = [(has_prev, dev(z_down, x, c)), (has_next, dev(z_up, x, c))]
+    others += [((x < 2) & has_prev, dev(z_down, at_x(2), c)), ((x >= 2) & has_next, dev(z_up, at_x(2), c))]
+    for is_there, peer in others:
+        pl.when(is_there)(functools.partial(greet, peer))
 
     own_src = [k_hbm.at[:, pl.ds(g * HD, HD)] for g in range(KV)]
     own_src += [v_hbm.at[:, pl.ds(g * HD, HD)] for g in range(KV)]
@@ -71,7 +81,7 @@
     for copy in own_copies:
         copy.start()
 
-    pl.semaphore_wait(barrier, len(peers))
+    pl.semaphore_wait(barrier, 6 + sum(is_there.astype(jnp.int32) for is_there, _ in others))
 
     def remote(src, dst, send, recv, device):
         return pltpu.make_async_remote_copy(
@@ -88,140 +98,100 @@
         remote(kv.at[slot, j], kv.at[slot, j], z_send.at[0, j], kv_recv.at[slot, j], sibling).wait_recv()
 
     started = [[] for _ in range(NX)]
-    OWN, PREV, RELAY = range(3)
+    OWN, PREV, RELAY, FAR_X = range(4)
     UP, DOWN = range(2)
 
-    def send(role, copy, *sem):
+    def guarded(condition, act):
+        if condition is None:
+            act()
+        else:
+            pl.when(condition)(act)
+
+    def send(role, condition, copy, *sem):
         copy.start()
-        started[role].append(sem)
-
-    def along_x(role, way, kind, src, dst, recv, j):
-        target = x_up if way == UP else x_down
-        send(role, remote(src, dst, x_send.at[way, kind, j], recv, target), x_send, way, kind, j)
-
-    def block_along_x(role, way, kind, origin, src, j):
+        started[role].append((condition, sem))
+
+    def along_x(role, condition, way, kind, src, dst, recv, j):
+        target = x_across if kind == FAR_X else x_up if way == UP else x_down
+        send(role, condition, remote(src, dst, x_send.at[way, kind, j], recv, target), x_send, way, kind, j)
+
+    def block_along_x(role, condition, way, kind, origin, src, j):
         slot = slots[origin]
-        along_x(role, way, kind, src, kv.at[slot, j], kv_recv.at[slot, j], j)
-
-    def to_sibling(role, origin, src, j):
-        send(role, sib_copy(src, origin, j), sib_send, origin, j)
-
-    def up_z(role, kind, origin, src, j):
-        slot = slots[origin]
-        send(role, remote(src, kv.at[slot, j], z_send.at[kind, j], kv_recv.at[slot, j], dev(z_up, x, c)), z_send, kind, j)
+        along_x(role, condition, way, kind, src, kv.at[slot, j], kv_recv.at[slot, j], j)
+
+    def up_z(role, kind, j):
+        slot = slots[role]
+        target = dev(z_up, at_x(2) if kind else x, c)
+        copy = remote(own_src[j], kv.at[slot, j], z_send.at[kind, j], kv_recv.at[slot, j], target)
+        send(role, has_next, copy, z_send, kind, j)
 
     def got(role, origin, j, *ways):
-        src = kv.at[slots[origin], j]
-        arrived(slots[origin], j)
-        for way in ways:
-            block_along_x(role, way, RELAY, origin, src, j)
-        to_sibling(role, origin, src, j)
+        condition = has_prev if origin > role else None
+
+        def act():
+            src = kv.at[slots[origin], j]
+            arrived(slots[origin], j)
+            for way in ways:
+                block_along_x(role, condition, way, RELAY, origin, src, j)
+            send(role, condition, sib_copy(src, origin, j), sib_send, origin, j)
+
+        guarded(condition, act)
 
     def got_prev(role, j, *ways):
-        src = kv.at[slots[role], j]
-        arrived(slots[role], j)
-        for way in ways:
-            block_along_x(role, way, PREV, role, src, j)
-
-        @pl.when(c == 1)
-        def _():
-            sib_copy(src, role, j).start()
-
-    def pass_on(role, which, origin, j):
-        remote(passing.at[which, j // 2], passing.at[which, j // 2], z_send.at[0, j], pass_recv.at[which, j // 2], sibling).wait_recv()
-        if which == 0:
-            block_along_x(role, DOWN, RELAY, origin, passing.at[which, j // 2], j)
-        else:
-            up_z(role, 1, origin, passing.at[which, j // 2], j)
-
-    def to_pass(role, way, kind, which, src, j):
-        along_x(role, way, kind, src, passing.at[which, j // 2], pass_recv.at[which, j // 2], j)
+        def act():
+            src = kv.at[slots[role], j]
+            arrived(slots[role], j)
+            for way in ways:
+                block_along_x(role, has_prev, way, PREV, role, src, j)
+
+            @pl.when(c == 1)
+            def _():
+                sib_copy(src, role, j).start()
+
+        guarded(has_prev, act)
 
     def own_sends(role, b):
+        for kind in (0, 1) if role >= 2 else (0,):
+            for j in (b, b + 1):
+                guarded(has_next, functools.partial(up_z, role, kind, j))
         for j in (b, b + 1):
             src = own_src[j]
-            up_z(role, 0, role, src, j)
-            if role == 1 and j == b:
-                to_pass(role, DOWN, OWN, 0, src, j)
             if role < 3:
-                block_along_x(role, UP, OWN, role, src, j)
+                block_along_x(role, None, UP, OWN, role, src, j)
             if role == 0:
-                block_along_x(role, DOWN, OWN, role, src, j)
+                block_along_x(role, None, DOWN, OWN, role, src, j)
 
             @pl.when(c == 0)
             def _():
                 sib_copy(src, role, j).start()
-
-    def stage_1(role, b):
-        if role == 0:
-            pass_on(0, 0, 1, b)
-            got_prev(0, b)
-        elif role == 1:
-            got(1, 0, b, UP)
-            got_prev(1, b, DOWN)
-        elif role == 2:
-            got_prev(2, b, DOWN)
-            got(2, 1, b)
-        else:
-            arrived(slots[2], b)
-            to_pass(3, UP, RELAY, 1, kv.at[slots[2], b], b)
-            to_sibling(3, 2, kv.at[slots[2], b], b)
-            got_prev(3, b, UP, DOWN)
-            got(3, 0, b)
-
-    def stage_2(role, b):
-        if role == 0:
-            pass_on(0, 1, 2, b)
-            got_prev(0, b + 1)
-        elif role == 1:
-            got_prev(1, b + 1, DOWN)
-            got(1, 0, b + 1)
-        elif role == 2:
-            got_prev(2, b + 1, DOWN)
-            got(2, 1, b + 1, UP)
-        else:
-            got_prev(3, b + 1, UP, DOWN)
-            got(3, 0, b + 1, DOWN)
-            got(3, 2, b + 1)
-
-    def stage_3(role, b):
-        if role == 0:
-            got(0, 3, b, UP)
-            got(0, 1, b)
-            got(0, 1, b + 1)
-            got(0, 2, b)
-        elif role == 1:
-            got(1, 2, b)
-            got(1, 2, b + 1, DOWN)
-        elif role == 2:
-            got(2, 3, b)
-            got(2, 3, b + 1, DOWN)
-            got(2, 0, b)
-        else:
-            got(3, 1, b)
-            got(3, 1, b + 1)
-
-    def stage_4(role, b):
-        if role == 0:
-            got(0, 3, b + 1)
-            got(0, 2, b + 1)
-        elif role == 1:
-            got(1, 3, b)
-            got(1, 3, b + 1)
-        elif role == 2:
-            got(2, 0, b + 1)
+        if role < 2:
+            for j in (b, b + 1):
+                block_along_x(role, None, UP, FAR_X, role, own_src[j], j)
+
+    def prev(role, j):
+        got_prev(role, j, *[[], [DOWN], [DOWN], [UP, DOWN]][role])
+
+    def others_x(role, j):
+        for d in (1, 3, 2):
+            got(role, (role + d) % NX, j)
 
     def in_role(stage, b):
         for role in range(NX):
-            @pl.when(x == role)
-            def _():
-                stage(role, b)
+            pl.when(x == role)(functools.partial(stage, role, b))
 
     in_role(own_sends, 0)
 
-    def from_sibling(j):
-        for d in (1, 3, 2):
-            arrived(at_x(d) * NC + 1 - c, j)
+    def there(slot):
+        return has_prev | (slot < i8)
+
+    def from_sibling(d, j):
+        slot = at_x(d) * NC + 1 - c
+        pl.when(there(slot))(lambda: arrived(slot, j))
+
+    for slot in range(ROW):
+        @pl.when(jnp.logical_not(there(slot)))
+        def _():
+            kv[slot] = jnp.zeros((2 * KV, T, HD), BF16)
 
     def w_start(i, carry):
         w_copy(i).start()
@@ -291,7 +261,7 @@
         return carry
 
     def close_scores(g, carry):
-        arrived(x * NC + 1 - c, g)
+        from_sibling(0, g)
         scores(1, 3, g)
         return carry
 
@@ -300,45 +270,44 @@
         return carry
 
     def other_scores(g, carry):
-        from_sibling(g)
+        for d in (1, 3, 2):
+            from_sibling(d, g)
         scores(6, 9, g)
-        return carry
-
-    def close_mix(g, carry):
-        arrived(x * NC + 1 - c, KV + g)
-        mix(0, g)
-        return carry
-
-    def same_mix(g, carry):
-        mix(3, g)
-        return carry
-
-    def other_mix(g, carry):
-        from_sibling(KV + g)
-        mix(6, g)
         return carry
 
     def each_kv(step):
         lax.fori_loop(0, KV, step, 0)
 
+    def close_mix(g):
+        from_sibling(0, KV + g)
+        mix(0, g)
+
+    def other_mix(g):
+        for d in (1, 3, 2):
+            from_sibling(d, KV + g)
+        mix(6, g)
+
+    in_role(prev, 0)
+    in_role(own_sends, KV)
     each_kv(own_scores)
-    in_role(stage_1, 0)
-    in_role(own_sends, KV)
-    in_role(stage_2, 0)
+    in_role(prev, 1)
     each_kv(close_scores)
-    in_role(stage_3, 0)
-    in_role(stage_1, KV)
-    in_role(stage_4, 0)
-    in_role(stage_2, KV)
+    in_role(others_x, 0)
+    in_role(prev, 2)
+    in_role(others_x, 1)
+    in_role(prev, 3)
     each_kv(same_scores)
     each_kv(other_scores)
     for h in range(HQ):
         top[h] = jnp.broadcast_to(jnp.max(top[h], axis=1, keepdims=True), (T, HD))
-    in_role(stage_3, KV)
-    each_kv(close_mix)
-    in_role(stage_4, KV)
-    each_kv(same_mix)
-    each_kv(other_mix)
+    close_mix(0)
+    in_role(others_x, 2)
+    mix(3, 0)
+    close_mix(1)
+    in_role(others_x, 3)
+    mix(3, 1)
+    other_mix(0)
+    other_mix(1)
 
     sums = jnp.zeros((T, HD), F32)
     for h in range(HQ):
@@ -380,8 +349,6 @@
         near_copy(i).start()
         return carry
 
-    lax.fori_loop(0, PIECES, send_near, 0)
-
     def combine(i, carry):
         target = jnp.where(lax.rem(i, 2) == 0, right, left)
         far_copy(i).wait_recv()
@@ -391,6 +358,7 @@
         return carry
 
     lax.fori_loop(0, PIECES, combine, 0)
+    lax.fori_loop(0, PIECES, send_near, 0)
 
     def add_up(i, carry):
         near_copy(i).wait_recv()
@@ -401,14 +369,26 @@
 
     lax.fori_loop(0, PIECES, add_up, 0)
 
-    for role in range(NX):
-        @pl.when(x == role)
-        def _():
-            for sems, *index in started[role]:
-                remote(kv.at[ROW, 0], kv.at[ROW, 0], sems.at[*index], kv_recv.at[0, 0], sibling).wait_send()
-
-    for j in range(2 * KV):
-        sib_copy(kv.at[i8, j], x, j).wait_send()
+    def sent(sems, *index):
+        remote(kv.at[ROW, 0], kv.at[ROW, 0], sems.at[*index], kv_recv.at[0, 0], sibling).wait_send()
+
+    def settle(role, _):
+        for condition in (None, has_prev, has_next):
+            todo = [sem for when, sem in started[role] if when is condition]
+
+            def act():
+                for sem in todo:
+                    sent(*sem)
+
+            if todo:
+                guarded(condition, act)
+
+    in_role(settle, 0)
+
+    @pl.when((c == 0) | has_prev)
+    def _():
+        for j in range(2 * KV):
+            sent(sib_send, x, j)
 
     def drain(i, carry):
         far_copy(i).wait_send()
@@ -443,7 +423,6 @@
         scratch_shapes=[
             pltpu.VMEM((T, HQ * HD), BF16),
             pltpu.VMEM((ROW + 1, 2 * KV, T, HD), BF16),
-            pltpu.VMEM((2, KV, T, HD), BF16),
             pltpu.VMEM((PIECES, HQ * HD, COLS), BF16),
             pltpu.VMEM((T, HD), BF16),
             pltpu.VMEM((ROW + 1, T, HD), BF16),
@@ -455,7 +434,7 @@
             pltpu.VMEM((2, PIECES, OWNED, COLS), BF16),
             pltpu.VMEM((PIECES, OWNED, COLS), BF16),
             dma, dma((2 * KV,)), dma((PIECES,)),
-            dma((2, 2 * KV)), dma((2, 3, 2 * KV)), dma((NX, 2 * KV)), dma((ROW, 2 * KV)), dma((2, KV)),
+            dma((2, 2 * KV)), dma((2, 4, 2 * KV)), dma((NX, 2 * KV)), dma((ROW, 2 * KV)),
             dma((PIECES,)), dma((PIECES,)), dma((2, PIECES)), dma((2, PIECES)),
         ],
         compiler_params=pltpu.CompilerParams(

time: 53.3 us -> 47.6 us (0.89)
  the two profiles are of different devices: /device:TPU:2 before, /device:TPU:128 now
where the time goes in v3:
time: 47.6 us; the launch traced here: 47.5 us
  Pallas kernels  46.9 us (99%)
  between operations  0.64 us (1%)
    pallas_call x1, Pallas kernels, local(): pl.pallas_call(kernel, out_shape=(pltpu.VMEM((T, HQ * HD), BF16), pltpu.V...  45.9 us
    pallas_call x1, Pallas kernels, local(): pl.pallas_call(hand_over, out_shape=tuple((jax.ShapeDtypeStruct(r.shape,...  1 us

profile of v3, /device:TPU:128, one launch (start us, length us, event | category | flops | bytes accessed | tf_op | source)
XLA Modules:
  0.0 47.5 jit_solution(17835137591350597685)
XLA Ops:
  0.6 45.9 %shard_map.76 = (bf16[256,1024]{1,0:T(8,128)(2,1)S(1)}, f32[8,256]{1,0:T(8,128)S(1)}, bf16[64,4096]{1,0:T(8,128)(2,1)S(1)}) custom-call(s32[16]{0:T(128)} %len_ref.1, bf16[256,1024]{1,0:T(8,128)(2,1)} %q_hbm.1, bf16[256,256]{1,0:T(8,128)(2,1)} %k_hbm.1, bf16[256,256]{1,0:T(8,128)(2,1)} %v_hbm.1, bf16[1024,4096]{1,0:T(8,128)(2,1)} %w_hbm.1), custom_call_target="tpu_custom_call" | custom-call | tf_op jit(solution)/shard_map/pallas_call | solution.py:414
  46.5 1.0 %shard_map.77 = (bf16[256,1024]{1,0:T(8,128)(2,1)}, f32[8,256]{1,0:T(8,128)}, bf16[64,4096]{1,0:T(8,128)(2,1)}) custom-call(bf16[256,1024]{1,0:T(8,128)(2,1)S(1)} %get-tuple-element.6.refs_0_, f32[8,256]{1,0:T(8,128)S(1)} %get-tuple-element.7.refs_1_, bf16[64,4096]{1,0:T(8,128)(2,1)S(1)} %get-tuple-element.8.refs_2_), custom_call_target="tpu_custom_call" | custom-call | tf_op jit(solution)/shard_map/pallas_call | solution.py:445

commit v4 on v3

--- a/solution.py
+++ b/solution.py
@@ -150,23 +150,25 @@
 
         guarded(has_prev, act)
 
-    def own_sends(role, b):
-        for kind in (0, 1) if role >= 2 else (0,):
-            for j in (b, b + 1):
-                guarded(has_next, functools.partial(up_z, role, kind, j))
-        for j in (b, b + 1):
-            src = own_src[j]
-            if role < 3:
-                block_along_x(role, None, UP, OWN, role, src, j)
-            if role == 0:
-                block_along_x(role, None, DOWN, OWN, role, src, j)
-
-            @pl.when(c == 0)
-            def _():
-                sib_copy(src, role, j).start()
-        if role < 2:
-            for j in (b, b + 1):
-                block_along_x(role, None, UP, FAR_X, role, own_src[j], j)
+    def own_sends(role, _):
+        for pair in ((0, 1), (2, 3)):
+            for kind in (0, 1) if role >= 2 else (0,):
+                for j in pair:
+                    guarded(has_next, functools.partial(up_z, role, kind, j))
+        for pair in ((0, 1), (2, 3)):
+            for j in pair:
+                src = own_src[j]
+                if role < 3:
+                    block_along_x(role, None, UP, OWN, role, src, j)
+                if role == 0:
+                    block_along_x(role, None, DOWN, OWN, role, src, j)
+
+                @pl.when(c == 0)
+                def _():
+                    sib_copy(src, role, j).start()
+            if role < 2:
+                for j in pair:
+                    block_along_x(role, None, UP, FAR_X, role, own_src[j], j)
 
     def prev(role, j):
         got_prev(role, j, *[[], [DOWN], [DOWN], [UP, DOWN]][role])
@@ -288,14 +290,13 @@
         mix(6, g)
 
     in_role(prev, 0)
-    in_role(own_sends, KV)
     each_kv(own_scores)
     in_role(prev, 1)
     each_kv(close_scores)
+    in_role(prev, 2)
     in_role(others_x, 0)
-    in_role(prev, 2)
+    in_role(prev, 3)
     in_role(others_x, 1)
-    in_role(prev, 3)
     each_kv(same_scores)
     each_kv(other_scores)
     for h in range(HQ):
@@ -306,15 +307,14 @@
     close_mix(1)
     in_role(others_x, 3)
     mix(3, 1)
+    def divide(g):
+        for h in range(g * GROUP, (g + 1) * GROUP):
+            att[:, head_columns(h)] = (acc[h, :, :HD] / acc[h, :, HD:]).astype(BF16)
+
     other_mix(0)
+    divide(0)
     other_mix(1)
-
-    sums = jnp.zeros((T, HD), F32)
-    for h in range(HQ):
-        total = acc[h, :, HD:]
-        att[:, h * HD : (h + 1) * HD] = (acc[h, :, :HD] / total).astype(BF16)
-        sums = jnp.where(lane == h, top[h] * SCALE + jnp.log(total), sums)
-    lse[...] = sums.T[:HQ]
+    divide(1)
 
     def rows(y):
         return pl.ds(pl.multiple_of(y * OWNED, OWNED), OWNED)
@@ -360,14 +360,10 @@
     lax.fori_loop(0, PIECES, combine, 0)
     lax.fori_loop(0, PIECES, send_near, 0)
 
-    def add_up(i, carry):
-        near_copy(i).wait_recv()
-        comb_copy(i).wait_recv()
-        mine = part[rows(me_y), pl.ds(column(i), COLS)].astype(F32)
-        proj[:, pl.ds(column(i), COLS)] = (mine + near[0, i].astype(F32) + near[1, i].astype(F32)).astype(BF16)
-        return carry
-
-    lax.fori_loop(0, PIECES, add_up, 0)
+    sums = jnp.zeros((T, HD), F32)
+    for h in range(HQ):
+        sums = jnp.where(lane == h, top[h] * SCALE + jnp.log(acc[h, :, HD:]), sums)
+    lse[...] = sums.T[:HQ]
 
     def sent(sems, *index):
         remote(kv.at[ROW, 0], kv.at[ROW, 0], sems.at[*index], kv_recv.at[0, 0], sibling).wait_send()
@@ -390,13 +386,20 @@
         for j in range(2 * KV):
             sent(sib_send, x, j)
 
-    def drain(i, carry):
+    def far_sent(i, carry):
         far_copy(i).wait_send()
-        near_copy(i).wait_send()
-        comb_copy(i).wait_send()
-        return carry
-
-    lax.fori_loop(0, PIECES, drain, 0)
+        return carry
+
+    lax.fori_loop(0, PIECES, far_sent, 0)
+
+    def add_up(i, carry):
+        comb_copy(i).wait()
+        near_copy(i).wait()
+        mine = part[rows(me_y), pl.ds(column(i), COLS)].astype(F32)
+        proj[:, pl.ds(column(i), COLS)] = (mine + near[0, i].astype(F32) + near[1, i].astype(F32)).astype(BF16)
+        return carry
+
+    lax.fori_loop(0, PIECES, add_up, 0)
 
 
 def hand_over(*refs):

time: 47.6 us -> 47.2 us (level)
  no operation moved by 1% of the time
where the time goes in v4:
time: 47.2 us; the launch traced here: 47.1 us
  Pallas kernels  46.5 us (99%)
  between operations  0.64 us (1%)
    pallas_call x1, Pallas kernels, local(): pl.pallas_call(kernel, out_shape=(pltpu.VMEM((T, HQ * HD), BF16), pltpu.V...  45.5 us
    pallas_call x1, Pallas kernels, local(): pl.pallas_call(hand_over, out_shape=tuple((jax.ShapeDtypeStruct(r.shape,...  1 us

profile of v4, /device:TPU:128, one launch (start us, length us, event | category | flops | bytes accessed | tf_op | source)
XLA Modules:
  0.0 47.1 jit_solution(6691360395453056639)
XLA Ops:
  0.6 45.5 %shard_map.76 = (bf16[256,1024]{1,0:T(8,128)(2,1)S(1)}, f32[8,256]{1,0:T(8,128)S(1)}, bf16[64,4096]{1,0:T(8,128)(2,1)S(1)}) custom-call(s32[16]{0:T(128)} %len_ref.1, bf16[256,1024]{1,0:T(8,128)(2,1)} %q_hbm.1, bf16[256,256]{1,0:T(8,128)(2,1)} %k_hbm.1, bf16[256,256]{1,0:T(8,128)(2,1)} %v_hbm.1, bf16[1024,4096]{1,0:T(8,128)(2,1)} %w_hbm.1), custom_call_target="tpu_custom_call" | custom-call | tf_op jit(solution)/shard_map/pallas_call | solution.py:417
  46.1 1.0 %shard_map.77 = (bf16[256,1024]{1,0:T(8,128)(2,1)}, f32[8,256]{1,0:T(8,128)}, bf16[64,4096]{1,0:T(8,128)(2,1)}) custom-call(bf16[256,1024]{1,0:T(8,128)(2,1)S(1)} %get-tuple-element.6.refs_0_, f32[8,256]{1,0:T(8,128)S(1)} %get-tuple-element.7.refs_1_, bf16[64,4096]{1,0:T(8,128)(2,1)S(1)} %get-tuple-element.8.refs_2_), custom_call_target="tpu_custom_call" | custom-call | tf_op jit(solution)/shard_map/pallas_call | solution.py:448

commit v5 on v4

--- a/solution.py
+++ b/solution.py
@@ -155,7 +155,6 @@
             for kind in (0, 1) if role >= 2 else (0,):
                 for j in pair:
                     guarded(has_next, functools.partial(up_z, role, kind, j))
-        for pair in ((0, 1), (2, 3)):
             for j in pair:
                 src = own_src[j]
                 if role < 3:
@@ -199,7 +198,6 @@
         w_copy(i).start()
         return carry
 
-    lax.fori_loop(0, PIECES, w_start, 0)
 
     lane = lax.broadcasted_iota(jnp.int32, (1, HD), 1)
     first = jnp.zeros((1, HD), jnp.int32)
@@ -295,6 +293,7 @@
     each_kv(close_scores)
     in_role(prev, 2)
     in_role(others_x, 0)
+    lax.fori_loop(0, PIECES, w_start, 0)
     in_role(prev, 3)
     in_role(others_x, 1)
     each_kv(same_scores)

time: 47.2 us -> 47.2 us (level)
  no operation moved by 1% of the time
where the time goes in v5:
time: 47.2 us; the launch traced here: 47.1 us
  Pallas kernels  46.5 us (99%)
  between operations  0.64 us (1%)
    pallas_call x1, Pallas kernels, local(): pl.pallas_call(kernel, out_shape=(pltpu.VMEM((T, HQ * HD), BF16), pltpu.V...  45.5 us
    pallas_call x1, Pallas kernels, local(): pl.pallas_call(hand_over, out_shape=tuple((jax.ShapeDtypeStruct(r.shape,...  1 us

profile of v5, /device:TPU:128, one launch (start us, length us, event | category | flops | bytes accessed | tf_op | source)
XLA Modules:
  0.0 47.1 jit_solution(14389313514734749109)
XLA Ops:
  0.6 45.5 %shard_map.76 = (bf16[256,1024]{1,0:T(8,128)(2,1)S(1)}, f32[8,256]{1,0:T(8,128)S(1)}, bf16[64,4096]{1,0:T(8,128)(2,1)S(1)}) custom-call(s32[16]{0:T(128)} %len_ref.1, bf16[256,1024]{1,0:T(8,128)(2,1)} %q_hbm.1, bf16[256,256]{1,0:T(8,128)(2,1)} %k_hbm.1, bf16[256,256]{1,0:T(8,128)(2,1)} %v_hbm.1, bf16[1024,4096]{1,0:T(8,128)(2,1)} %w_hbm.1), custom_call_target="tpu_custom_call" | custom-call | tf_op jit(solution)/shard_map/pallas_call | solution.py:416
  46.1 1.0 %shard_map.77 = (bf16[256,1024]{1,0:T(8,128)(2,1)}, f32[8,256]{1,0:T(8,128)}, bf16[64,4096]{1,0:T(8,128)(2,1)}) custom-call(bf16[256,1024]{1,0:T(8,128)(2,1)S(1)} %get-tuple-element.6.refs_0_, f32[8,256]{1,0:T(8,128)S(1)} %get-tuple-element.7.refs_1_, bf16[64,4096]{1,0:T(8,128)(2,1)S(1)} %get-tuple-element.8.refs_2_), custom_call_target="tpu_custom_call" | custom-call | tf_op jit(solution)/shard_map/pallas_call | solution.py:447
